TPU v7x, 32 devices: a whole 2x2x4 slice. The times are simulated.
32 devices in a mesh: parts: 2 (over x), expert: 16 (over z, y, core).
Axes of the slice: x: 2, y: 2, z: 4, core: 2. Of those that a mesh axis runs over, the one named last changes fastest.
Arguments:
- queries: bfloat16 [3072, 2048], P(('parts', 'expert')), parts along dimension 0, may hold values from -150 to 150
- kv_cache: bfloat16 [6144, 16, 512], P(('parts', 'expert')), parts along dimension 0, may hold values from -6 to 6
- new_kv: bfloat16 [3072, 512], P(('parts', 'expert')), parts along dimension 0, may hold values from -6 to 6
- page_table: int32 [3072, 16], P(('parts', 'expert')), parts along dimension 0, may hold values from 0 to 191, as said below
- ctx_len: int32 [3072], P(('parts', 'expert')), parts along dimension 0, may hold values from 2 to 256, as said below
- resid: bfloat16 [3072, 1024], P(('parts', 'expert')), parts along dimension 0, may hold values from -6 to 6
- w_out: bfloat16 [2048, 1024], replicated, may hold values from -0.125 to 0.125
- moe_gain: float32 [1024], replicated, may hold values from 0.25 to 1.75
- w_gate: bfloat16 [16, 1024, 768], P('expert'), may hold values from -0.1875 to 0.1875
- w_up: bfloat16 [16, 1024, 768], P('expert'), may hold values from -0.1875 to 0.1875
- w_down: bfloat16 [16, 768, 1024], P('expert'), may hold values from -0.21875 to 0.21875
- routes: int32 [3072, 8], P(('parts', 'expert')), parts along dimension 0, may hold values from 0 to 15, all different within a row; in each aligned block of 48 rows (0 to 47, 48 to 95, ...) at most 48 rows name the same one
- route_weight: float32 [3072, 8], P(('parts', 'expert')), parts along dimension 0, may hold values from 0.05 to 0.3
- talker_owner: int32 [3072], P(('parts', 'expert')), parts along dimension 0, may hold values from 0 to 15, as said below
- speaking: int32 [3072], P(('parts', 'expert')), parts along dimension 0, may hold values from 0 to 1
- codec_state: bfloat16 [3072, 1024], P(('parts', 'expert')), parts along dimension 0, may hold values from -6 to 6
- talk_gain: float32 [1024], replicated, may hold values from 0.25 to 1.75
- w_talk: bfloat16 [1024, 1024], replicated, may hold values from -0.1875 to 0.1875
Outputs:
- thinker_out: bfloat16 [3072, 1024], P(('parts', 'expert')), parts along dimension 0
- talker_out: bfloat16 [3072, 1024], P(('parts', 'expert')), parts along dimension 0
There are 2 independent parts, one for each index of `parts`. A program takes and returns all parts, laid end to end along the dimension named above; an argument that names none is the same for every part. Nothing has to cross between parts.
Inputs may be any that keep to these rules, and one draw needn't show every extreme that they name: `page_table`: entries j < ceil(ctx_len[r] / 16) name pages of the pool of the device that holds request r, counted within that pool; live pages of different requests differ; other entries are 0. `ctx_len`: in every draw some request has 256 cached tokens. `routes`: each row names 8 different experts. In each aligned block of 48 rows no expert is named by more than 48 rows, and some block reaches that. `talker_owner`: among the speaking rows of one device at most 6 have the same owner; a device's rows are spread over the owners as evenly as possible, and some owner receives exactly 6 speaking rows from every device.
All inputs are finite; a program needn't handle non-finite values.
Results may differ from a plain program's by a relative error of at most 0.01.
Values may be sent and summed in bfloat16 or wider, within the bound.
A program may use at most 192 MiB of HBM per device.

v0:
```python
import functools
import math

import jax
import jax.numpy as jnp
from jax import lax
from jax.experimental import pallas as pl
from jax.experimental.pallas import tpu as pltpu
from jax.sharding import PartitionSpec as P

HD = 128
STACK = 4
NEG = -1e30
LOG2E = 1.4426950408889634


def attend_kernel(
    kv_heads,
    page,
    q_ref,
    kv_ref,
    fresh_ref,
    table_ref,
    len_ref,
    resid_ref,
    wout_ref,
    gain_ref,
    hidden_ref,
    normed_ref,
    bias_ref,
    att_ref,
):
    rows, qwidth = q_ref.shape
    tokens = kv_ref.shape[0]
    pages = tokens // page
    max_pages = table_ref.shape[1]
    heads = qwidth // HD
    per_kv = heads // kv_heads
    factor = LOG2E / math.sqrt(HD)

    lengths = len_ref[...]
    page_ids = lax.broadcasted_iota(jnp.int32, (rows, pages), 1)
    whole = jnp.zeros((rows, pages), jnp.float32)
    last = jnp.zeros((rows, pages), jnp.float32)
    for j in range(max_pages):
        named = page_ids == table_ref[:, j : j + 1]
        whole += jnp.where(named & (lengths >= page * (j + 1)), 1.0, 0.0)
        last += jnp.where(
            named & (lengths > page * j) & (lengths < page * (j + 1)), 1.0, 0.0
        )
    spread = jnp.where(
        lax.broadcasted_iota(jnp.int32, (pages, tokens), 1) // page
        == lax.broadcasted_iota(jnp.int32, (pages, tokens), 0),
        1.0,
        0.0,
    ).astype(jnp.bfloat16)
    whole_tok = jnp.dot(whole.astype(jnp.bfloat16), spread, preferred_element_type=jnp.float32)
    last_tok = jnp.dot(last.astype(jnp.bfloat16), spread, preferred_element_type=jnp.float32)
    place = lax.rem(lax.broadcasted_iota(jnp.int32, (rows, tokens), 1), page)
    times = whole_tok + jnp.where(place < lax.rem(lengths, page), last_tok, 0.0)
    bias_ref[...] = jnp.where(times > 0.5, jnp.log2(jnp.maximum(times, 1.0)), NEG)

    def step(i, carry):
        kvh = (i * STACK) // per_kv
        lanes = pl.ds(pl.multiple_of(i * STACK * HD, STACK * HD), STACK * HD)
        keys = pl.ds(pl.multiple_of(kvh * HD, HD), HD)
        vals = pl.ds(pl.multiple_of((kv_heads + kvh) * HD, HD), HD)
        qs = q_ref[:, lanes]
        stacked = jnp.concatenate([qs[:, h * HD : (h + 1) * HD] for h in range(STACK)], axis=0)
        scores = lax.dot_general(
            stacked, kv_ref[:, keys], (((1,), (1,)), ((), ())), preferred_element_type=jnp.float32
        )
        fresh_key = fresh_ref[:, keys].astype(jnp.float32)
        fresh_val = fresh_ref[:, vals].astype(jnp.float32)
        wide = stacked.astype(jnp.float32).reshape(STACK, rows, HD)
        own = jnp.sum(wide * fresh_key[None], axis=-1, keepdims=True) * factor
        logits = scores.reshape(STACK, rows, tokens) * factor + bias_ref[...][None]
        highest = jnp.maximum(jnp.max(logits, axis=-1, keepdims=True), own)
        weights = jnp.exp2(logits - highest)
        own_weight = jnp.exp2(own - highest)
        denom = jnp.sum(weights, axis=-1, keepdims=True) + own_weight
        mixed = jnp.dot(
            weights.astype(jnp.bfloat16).reshape(STACK * rows, tokens),
            kv_ref[:, vals],
            preferred_element_type=jnp.float32,
        ).reshape(STACK, rows, HD)
        mixed = ((mixed + own_weight * fresh_val[None]) / denom).astype(jnp.bfloat16)
        att_ref[:, lanes] = jnp.concatenate([mixed[h] for h in range(STACK)], axis=1)
        return carry

    lax.fori_loop(0, heads // STACK, step, 0)
    hidden = (
        resid_ref[...].astype(jnp.float32)
        + jnp.dot(att_ref[...], wout_ref[...], preferred_element_type=jnp.float32)
    ).astype(jnp.bfloat16)
    hidden_ref[...] = hidden
    normed_ref[...] = rms_scaled(hidden, gain_ref[...]).astype(jnp.bfloat16)


def rms_scaled(values, gain_row):
    widened = values.astype(jnp.float32)
    return (
        widened * lax.rsqrt(jnp.mean(widened * widened, axis=-1, keepdims=True) + 1e-06) * gain_row
    )


def attend(queries, kv_cache, new_kv, page_table, ctx_len, resid, w_out, moe_gain):
    rows, width = resid.shape
    pages, page, kv_width = kv_cache.shape
    tokens = pages * page
    shape = jax.ShapeDtypeStruct((rows, width), jnp.bfloat16)
    return pl.pallas_call(
        functools.partial(attend_kernel, kv_width // (2 * HD), page),
        out_shape=(shape, shape),
        in_specs=[pl.BlockSpec(memory_space=pltpu.VMEM)] * 8,
        out_specs=(pl.BlockSpec(memory_space=pltpu.VMEM),) * 2,
        scratch_shapes=[
            pltpu.VMEM((rows, tokens), jnp.float32),
            pltpu.VMEM((rows, queries.shape[1]), jnp.bfloat16),
        ],
        compiler_params=pltpu.CompilerParams(vmem_limit_bytes=48 * 1024 * 1024),
        cost_estimate=pl.CostEstimate(
            flops=4 * rows * queries.shape[1] * tokens,
            bytes_accessed=2 * (tokens * kv_width + w_out.size + 4 * resid.size),
            transcendentals=0,
        ),
    )(
        queries,
        kv_cache.reshape(tokens, kv_width),
        new_kv,
        page_table,
        ctx_len[:, None],
        resid,
        w_out,
        moe_gain[None, :],
    )


def talker_pick(owners, voiced, devices, capacity):
    row_total = owners.shape[0]
    one_hot = (owners[:, None] == jnp.arange(devices, dtype=jnp.int32)[None, :]) & (
        voiced[:, None] == 1
    )
    order = jnp.arange(row_total, dtype=jnp.int32)
    before = (order[None, :] < order[:, None]).astype(jnp.bfloat16)
    counts = jnp.dot(before, one_hot.astype(jnp.bfloat16), preferred_element_type=jnp.float32)
    earlier = jnp.sum(jnp.where(one_hot, counts, 0.0), axis=1).astype(jnp.int32)
    target = jnp.where(voiced == 1, owners * capacity + earlier, devices * capacity)
    slots = jnp.arange(devices * capacity, dtype=jnp.int32)
    return (slots[:, None] == target[None, :]).astype(jnp.bfloat16)


def body(
    queries,
    kv_cache,
    new_kv,
    page_table,
    ctx_len,
    resid,
    w_out,
    moe_gain,
    w_gate,
    w_up,
    w_down,
    routes,
    route_weight,
    talker_owner,
    speaking,
    codec_state,
    talk_gain,
    w_talk,
):
    devices = lax.axis_size("expert")
    capacity = codec_state.shape[0] // devices
    local = w_gate.shape[0]
    experts = local * devices
    width = resid.shape[1]
    dense = jnp.sum(
        jnp.where(
            routes[:, :, None] == jnp.arange(experts, dtype=jnp.int32)[None, None, :],
            route_weight[:, :, None],
            0.0,
        ),
        axis=1,
    )
    dense_all = lax.all_gather(dense, "expert", axis=0, tiled=True)
    hidden, normed = attend(
        queries, kv_cache, new_kv, page_table, ctx_len, resid, w_out, moe_gain
    )
    everyone = lax.all_gather(normed, "expert", axis=0, tiled=True)
    me = lax.axis_index("expert")
    partial = 0.0
    for e in range(local):
        mine = jnp.arange(experts, dtype=jnp.int32) == me * local + e
        scale = jnp.sum(jnp.where(mine[None, :], dense_all, 0.0), axis=1, keepdims=True)
        gate_values = jnp.dot(everyone, w_gate[e], preferred_element_type=jnp.float32)
        up_values = jnp.dot(everyone, w_up[e], preferred_element_type=jnp.float32)
        activated = (jax.nn.silu(gate_values) * up_values).astype(jnp.bfloat16)
        partial = partial + scale * jnp.dot(
            activated, w_down[e], preferred_element_type=jnp.float32
        )
    mixture = lax.psum_scatter(
        partial.astype(jnp.bfloat16), "expert", scatter_dimension=0, tiled=True
    )
    thinker_out = (hidden.astype(jnp.float32) + mixture.astype(jnp.float32)).astype(jnp.bfloat16)
    voice_in = rms_scaled(thinker_out, talk_gain).astype(jnp.bfloat16)
    pick = talker_pick(talker_owner, speaking, devices, capacity)
    outgoing_voice = (
        jnp.dot(pick, voice_in, preferred_element_type=jnp.float32)
        .astype(jnp.bfloat16)
        .reshape(devices, capacity, width)
    )
    arrived = lax.all_to_all(outgoing_voice, "expert", split_axis=0, concat_axis=0, tiled=True)
    projected = jnp.dot(
        arrived.reshape(devices * capacity, width), w_talk, preferred_element_type=jnp.float32
    )
    talker_out = (codec_state.astype(jnp.float32) + projected).astype(jnp.bfloat16)
    return (thinker_out, talker_out)


def solution(mesh):
    both = ("parts", "expert")
    in_specs = (
        P(both, None),
        P(both, None, None),
        P(both, None),
        P(both, None),
        P(both),
        P(both, None),
        P(),
        P(),
        P("expert", None, None),
        P("expert", None, None),
        P("expert", None, None),
        P(both, None),
        P(both, None),
        P(both),
        P(both),
        P(both, None),
        P(),
        P(),
    )
    out_specs = (P(both, None), P(both, None))
    return jax.shard_map(body, mesh=mesh, in_specs=in_specs, out_specs=out_specs, check_vma=False)
```

profile of v0, /device:TPU:0, one launch (start us, length us, event | category | flops | bytes accessed | tf_op | source)
XLA Modules:
  0.0 183.5 jit_solution(14004424548935929857)
XLA Ops:
  7.2 0.9 copy.37.table_ref
  8.2 0.8 copy.38.len_ref
  8.9 1.9 %copy-done.1 = bf16[192,16,512]{2,1,0:T(8,128)(2,1)S(1)} copy-done((bf16[192,16,512]{2,1,0:T(8,128)(2,1)S(1)}, bf16[192,16,512]{2,1,0:T(8,128)(2,1)}, u32[]{:S(2)}) %copy-start.1) | copy-done | bytes 3145752
  10.8 1.0 copy-done.2
  11.8 0.9 copy-done.3
  12.7 0.9 copy-done.4
  13.6 0.7 copy-done.5
  14.3 14.4 %shard_map.185 = (bf16[96,1024]{1,0:T(8,128)(2,1)S(1)}, bf16[96,1024]{1,0:T(8,128)(2,1)}) custom-call(bf16[96,2048]{1,0:T(8,128)(2,1)S(1)} %copy-done.2, bf16[3072,512]{1,0:T(8,128)(2,1)S(1)} %bitcast.21, bf16[96,512]{1,0:T(8,128)(2,1)S(1)} %copy-done.4, s32[96,16]{1,0:T(8,128)S(1)} %copy.37.table_ref, s32[96,1]{1,0:T(8,128)S(1)} %copy.38.len_ref, ...), custom_call_target="tpu_custom_call" | custom-call | flops 2415919104 | bytes 8126464 | tf_op jit(solution)/shard_map/pallas_call | solution.py:112
  28.8 0.0 reduce-scatter.2.cloned.1.call-start
  28.9 23.6 %all-gather = f32[16,96,16]{1,2,0:T(8,128)S(1)} all-gather(f32[1,96,16]{1,2,0:T(8,128)S(1)} %bitcast.23), channel_id=1, replica_groups=mesh['parts'=2,'expert'=16] {'expert'}, dimensions={0}, use_global_device_ids=true | all-gather | bytes 104448 | tf_op jit(solution)/shard_map/all_gather | solution.py:186
  52.5 0.1 reshape.37
  52.6 0.1 select_reduce_fusion
  52.7 24.4 %all-gather.3.cloned.1.call-done = bf16[1536,1024]{1,0:T(8,128)(2,1)} async-done(((bf16[96,1024]{1,0:T(8,128)(2,1)}), bf16[1536,1024]{1,0:T(8,128)(2,1)}) %all-gather.3.cloned.1.call-update) | async-done | bytes 3145744 | tf_op jit(solution)/shard_map/all_gather | solution.py:190
  77.1 7.1 %fusion.2 = f32[1536,768]{1,0:T(8,128)} fusion(bf16[1536,1024]{1,0:T(8,128)(2,1)} %all-gather.3.cloned.1.call-done, bf16[1,1024,768]{2,1,0:T(8,128)(2,1)} %param.26), kind=kOutput, calls=%fused_computation.4 | convolution fusion | flops 2415919104 | bytes 9437184 | tf_op jit(solution)/shard_map/dot_general | solution.py:196
  84.2 10.9 %multiply_convert_fusion = bf16[1536,1024]{1,0:T(8,128)(2,1)} fusion(f32[1536]{0:T(1024)S(1)} %select_reduce_fusion, bf16[1,768,1024]{2,1,0:T(8,128)(2,1)} %param.28, f32[1536,768]{1,0:T(8,128)} %fusion.2, bf16[1536,1024]{1,0:T(8,128)(2,1)} %all-gather.3.cloned.1.call-done, bf16[1,1024,768]{2,1,0:T(8,128)(2,1)} %param.27), kind=kOutput, calls=%fused_computation | convolution fusion | flops 4842061824 | bytes 14161920 | tf_op jit(solution)/shard_map/dot_general | solution.py:199
  95.1 0.6 copy-done.12
  95.7 0.2 fusion.7
  95.9 64.4 %reduce-scatter.2.cloned.1.call-done = bf16[96,1024]{1,0:T(8,128)(2,1)} async-done(((bf16[1536,1024]{1,0:T(8,128)(2,1)}), bf16[96,1024]{1,0:T(8,128)(2,1)}) %reduce-scatter.2.cloned.1.call-update) | async-done | bytes 196624 | tf_op jit(solution)/shard_map/reduce_scatter | solution.py:202
  160.3 1.1 fusion.8
  161.5 0.3 convolution_convert_fusion
  161.7 0.1 reshape.34
  161.8 13.5 %all_to_all.5 = bf16[16,6,1024]{2,1,0:T(8,128)(2,1)S(1)} all-to-all(bf16[16,6,1024]{2,1,0:T(8,128)(2,1)S(1)} %reshape.34), channel_id=1, replica_groups=mesh['parts'=2,'expert'=16] {'expert'}, dimensions={0} | all-to-all | bytes 393216 | tf_op jit(solution)/shard_map/all_to_all | solution.py:213
  175.4 0.1 reshape.35
  175.5 1.2 fusion.6
  (29 shorter events, 0.2 us)
Async XLA Ops:
  7.2 168.3 %copy-start = (bf16[1024,1024]{1,0:T(8,128)(2,1)S(1)}, bf16[1024,1024]{1,0:T(8,128)(2,1)}, u32[]{:S(2)}) copy-start(bf16[1024,1024]{1,0:T(8,128)(2,1)} %param.35) | copy-start | bytes 6291460
  7.2 69.9 %all-gather.3.cloned.1.call-start = ((), (), s32[]{:S(2)}) async-start(), calls=%async_computation.2 | async-start | bytes 3342336 | tf_op jit(solution)/shard_map/all_gather | solution.py:190
  8.9 1.9 %copy-start.1 = (bf16[192,16,512]{2,1,0:T(8,128)(2,1)S(1)}, bf16[192,16,512]{2,1,0:T(8,128)(2,1)}, u32[]{:S(2)}) copy-start(bf16[192,16,512]{2,1,0:T(8,128)(2,1)} %param.19) | copy-start | bytes 9437188
  10.8 1.0 copy-start.2
  11.8 0.9 copy-start.3
  12.7 0.9 copy-start.4
  13.6 0.7 copy-start.5
  14.3 14.5 %copy-start.9 = (f32[96,8]{0,1:T(8,128)S(1)}, f32[96,8]{0,1:T(8,128)}, u32[]{:S(2)}) copy-start(f32[96,8]{0,1:T(8,128)} %param.30) | copy-start | bytes 9220
  14.3 14.5 %copy-start.10 = (s32[96,8]{0,1:T(8,128)S(1)}, s32[96,8]{0,1:T(8,128)}, u32[]{:S(2)}) copy-start(s32[96,8]{0,1:T(8,128)} %param.29) | copy-start | bytes 9220
  28.8 131.6 %reduce-scatter.2.cloned.1.call-start = ((), (), s32[]{:S(2)}) async-start(), calls=%async_computation.3 | async-start | bytes 3342336 | tf_op jit(solution)/shard_map/reduce_scatter | solution.py:202
  95.1 0.7 copy-start.12
  95.1 0.7 copy-start.11
  95.1 66.4 %copy-start.8 = (f32[1024]{0:T(1024)S(1)}, f32[1024]{0:T(1024)}, u32[]{:S(2)}) copy-start(f32[1024]{0:T(1024)} %param.34) | copy-start | bytes 12292
  95.1 80.4 %copy-start.7 = (bf16[96,1024]{1,0:T(8,128)(2,1)S(1)}, bf16[96,1024]{1,0:T(8,128)(2,1)}, u32[]{:S(2)}) copy-start(bf16[96,1024]{1,0:T(8,128)(2,1)} %param.33) | copy-start | bytes 589828
  161.4 15.2 %copy-start.6 = (bf16[96,1024]{1,0:T(8,128)(2,1)}, bf16[96,1024]{1,0:T(8,128)(2,1)S(1)}, u32[]{:S(2)}) copy-start(bf16[96,1024]{1,0:T(8,128)(2,1)S(1)} %get-tuple-element.7) | copy-start | bytes 589828
Sparse Core Ops, SparseCore 0:
  28.9 48.1 all-gather.2
  95.2 65.0 reduce-scatter.1
where the time goes:
time: 184 us; the launch traced here: 183 us
  waiting for transfers between devices  88.8 us (48%)
  blocking collectives  37.1 us (20%)
  matrix products  19.6 us (11%)
  Pallas kernels  14.4 us (8%)
  between operations  14.2 us (8%)
  local copies, waits for them, and re-layouts  8.01 us (4%)
    reduce_scatter x1, waiting for transfers between devices, body(): lax.psum_scatter(partial.astype(jnp.bfloat16), 'expert', scatter_dimensio...  64.4 us
    all_gather x1, waiting for transfers between devices, body(): everyone = lax.all_gather(normed, 'expert', axis=0, tiled=True)  24.4 us
    all_gather x1, blocking collectives, body(): dense_all = lax.all_gather(dense, 'expert', axis=0, tiled=True)  23.6 us
    pallas_call x1, Pallas kernels, attend(): pl.pallas_call(functools.partial(attend_kernel, kv_width // (2 * HD), pag...  14.4 us
    all_to_all x1, blocking collectives, body(): lax.all_to_all(outgoing_voice, 'expert', split_axis=0, concat_axis=0, til...  13.5 us
    dot_general x1, matrix products, body(): jnp.dot(activated, w_down[e], preferred_element_type=jnp.float32)  10.9 us
    dot_general x1, matrix products, body(): jnp.dot(everyone, w_gate[e], preferred_element_type=jnp.float32)  7.1 us
    unnamed x28, local copies, waits for them, and re-layouts  7.07 us
  transfers between devices with their start and end apart: 2, of which 2 were waited for; matrix products, arithmetic and copies ran while one was open for 0% of the time, Pallas kernels for 0%

commit v1 on v0

--- a/solution.py
+++ b/solution.py
@@ -136,8 +136,171 @@
     )
 
 
-def talker_pick(owners, voiced, devices, capacity):
+def flipped(me, bits, total):
+    out, stride = 0, 1
+    while stride < total:
+        bit = (me // stride) % 2
+        out = out + stride * ((1 - bit) if bits & stride else bit)
+        stride *= 2
+    return out
+
+
+def finish_kernel(
+    n,
+    capacity,
+    part_ref,
+    hidden_ref,
+    picks_ref,
+    gain_ref,
+    codec_ref,
+    wtalk_ref,
+    thinker_ref,
+    talker_ref,
+    stage,
+    landed,
+    voice_out,
+    voice_in,
+    send_sem,
+    recv_sem,
+    voice_send,
+    voice_recv,
+):
+    rows, width = hidden_ref.shape
+    cols = width // 2
+    room = voice_out.shape[1]
+    me = lax.axis_index("expert")
+    barrier = pltpu.get_barrier_semaphore()
+
+    def greet(i, carry):
+        peer = (me + i) % n
+        pl.semaphore_signal(
+            barrier, inc=1, device_id={"expert": peer}, device_id_type=pl.DeviceIdType.MESH
+        )
+        return carry
+
+    lax.fori_loop(1, n, greet, 0)
+    pl.semaphore_wait(barrier, n - 1)
+
+    strides = [1 << b for b in range(n.bit_length() - 1)]
+    orders = (strides, strides[:1] + strides[2:] + strides[1:2])
+
+    def step_of(half, r):
+        return next(k for k, s in enumerate(orders[half]) if r & s)
+
+    def message(half, r, source):
+        partner = flipped(me, orders[half][step_of(half, r)], n)
+        return pltpu.make_async_remote_copy(
+            src_ref=source,
+            dst_ref=landed.at[half, r],
+            send_sem=send_sem.at[half, r],
+            recv_sem=recv_sem.at[half, r],
+            device_id={"expert": partner},
+            device_id_type=pl.DeviceIdType.MESH,
+        )
+
+    def summed(half, r, k):
+        lanes = slice(half * cols, (half + 1) * cols)
+        total = part_ref[flipped(me, r, n), :, lanes].astype(jnp.float32)
+        for j in range(k):
+            m = r + orders[half][j]
+            sent[half, m].wait_recv()
+            total = total + landed[half, m].astype(jnp.float32)
+        return total
+
+    sent = {}
+    for k in range(len(strides)):
+        for half in range(2):
+            todo = [r for r in range(1, n) if step_of(half, r) == k]
+            nearer = orders[half][k + 1 :]
+            todo.sort(key=lambda r: [-((r & s) > 0) for s in nearer])
+            for r in todo:
+                if k == 0:
+                    source = part_ref.at[flipped(me, r, n), :, pl.ds(half * cols, cols)]
+                else:
+                    stage[half, r] = summed(half, r, k).astype(jnp.bfloat16)
+                    source = stage.at[half, r]
+                sent[half, r] = message(half, r, source)
+                sent[half, r].start()
+    mixture = jnp.concatenate([summed(half, 0, len(strides)) for half in range(2)], axis=1)
+    thinker = (hidden_ref[...].astype(jnp.float32) + mixture).astype(jnp.bfloat16)
+    thinker_ref[...] = thinker
+    voice = rms_scaled(thinker, gain_ref[...]).astype(jnp.bfloat16)
+    packed = jnp.dot(picks_ref[0], voice[:, :cols], preferred_element_type=jnp.float32) + jnp.dot(
+        picks_ref[1], voice[:, cols:], preferred_element_type=jnp.float32
+    )
+    voice_out[...] = packed.astype(jnp.bfloat16).reshape(n, room, cols)
+    voice_in[pl.ds(me, 1)] = voice_out[pl.ds(me, 1)]
+
+    def voice_copy(i):
+        peer = (me + i) % n
+        return pltpu.make_async_remote_copy(
+            src_ref=voice_out.at[peer],
+            dst_ref=voice_in.at[me],
+            send_sem=voice_send.at[i],
+            recv_sem=voice_recv.at[i],
+            device_id={"expert": peer},
+            device_id_type=pl.DeviceIdType.MESH,
+        )
+
+    def begin(i, carry):
+        voice_copy(i).start()
+        return carry
+
+    def end(i, carry):
+        copy = voice_copy(i)
+        copy.wait_send()
+        copy.wait_recv()
+        return carry
+
+    lax.fori_loop(1, n, begin, 0)
+    for copy in sent.values():
+        copy.wait_send()
+    lax.fori_loop(1, n, end, 0)
+    arrived = voice_in[...].reshape(n * room, cols)
+    slot = lax.broadcasted_iota(jnp.int32, (n * capacity, n * room), 0)
+    place = lax.broadcasted_iota(jnp.int32, (n * capacity, n * room), 1)
+    near = (slot // capacity) * room + lax.rem(slot, capacity)
+    total = codec_ref[...].astype(jnp.float32)
+    for half in range(2):
+        chosen = jnp.where(place == near + half * (room // 2), 1.0, 0.0).astype(jnp.bfloat16)
+        part = jnp.dot(chosen, arrived, preferred_element_type=jnp.float32).astype(jnp.bfloat16)
+        total = total + jnp.dot(
+            part, wtalk_ref[half * cols : (half + 1) * cols, :], preferred_element_type=jnp.float32
+        )
+    talker_ref[...] = total.astype(jnp.bfloat16)
+
+
+def finish(n, capacity, partial, hidden, picks, talk_gain, codec_state, w_talk):
+    rows, width = hidden.shape
+    room = picks.shape[1] // n
+    cols = width // 2
+    return pl.pallas_call(
+        functools.partial(finish_kernel, n, capacity),
+        out_shape=(
+            jax.ShapeDtypeStruct((rows, width), jnp.bfloat16),
+            jax.ShapeDtypeStruct(codec_state.shape, jnp.bfloat16),
+        ),
+        in_specs=[pl.BlockSpec(memory_space=pltpu.VMEM)] * 6,
+        out_specs=(pl.BlockSpec(memory_space=pltpu.VMEM),) * 2,
+        scratch_shapes=[
+            pltpu.VMEM((2, n, rows, cols), jnp.bfloat16),
+            pltpu.VMEM((2, n, rows, cols), jnp.bfloat16),
+            pltpu.VMEM((n, room, cols), jnp.bfloat16),
+            pltpu.VMEM((n, room, cols), jnp.bfloat16),
+            pltpu.SemaphoreType.DMA((2, n)),
+            pltpu.SemaphoreType.DMA((2, n)),
+            pltpu.SemaphoreType.DMA((n,)),
+            pltpu.SemaphoreType.DMA((n,)),
+        ],
+        compiler_params=pltpu.CompilerParams(
+            collective_id=0, has_side_effects=True, vmem_limit_bytes=56 * 1024 * 1024
+        ),
+    )(partial.reshape(n, rows, width), hidden, picks, talk_gain[None, :], codec_state, w_talk)
+
+
+def talker_picks(owners, voiced, devices, capacity):
     row_total = owners.shape[0]
+    span = -(-capacity // 8) * 8
     one_hot = (owners[:, None] == jnp.arange(devices, dtype=jnp.int32)[None, :]) & (
         voiced[:, None] == 1
     )
@@ -145,9 +308,15 @@
     before = (order[None, :] < order[:, None]).astype(jnp.bfloat16)
     counts = jnp.dot(before, one_hot.astype(jnp.bfloat16), preferred_element_type=jnp.float32)
     earlier = jnp.sum(jnp.where(one_hot, counts, 0.0), axis=1).astype(jnp.int32)
-    target = jnp.where(voiced == 1, owners * capacity + earlier, devices * capacity)
-    slots = jnp.arange(devices * capacity, dtype=jnp.int32)
-    return (slots[:, None] == target[None, :]).astype(jnp.bfloat16)
+    room = 2 * span
+    target = jnp.where(voiced == 1, owners * room + earlier, -room)
+    slots = jnp.arange(devices * room, dtype=jnp.int32)
+    return jnp.stack(
+        [
+            (slots[:, None] == target[None, :] + half * span).astype(jnp.bfloat16)
+            for half in range(2)
+        ]
+    )
 
 
 def body(
@@ -183,39 +352,40 @@
         ),
         axis=1,
     )
-    dense_all = lax.all_gather(dense, "expert", axis=0, tiled=True)
+    coarse = lax.reduce_precision(dense, 8, 7)
+    wide = -(-2 * experts // 128) * 128
+    riders = jnp.concatenate([coarse, dense - coarse], axis=1).astype(jnp.bfloat16)
+    riders = jnp.pad(riders, ((0, 0), (0, wide - 2 * experts)))
+    picks = talker_picks(talker_owner, speaking, devices, capacity)
     hidden, normed = attend(
         queries, kv_cache, new_kv, page_table, ctx_len, resid, w_out, moe_gain
     )
-    everyone = lax.all_gather(normed, "expert", axis=0, tiled=True)
+    gathered = lax.all_gather(
+        jnp.concatenate([normed, riders], axis=1), "expert", axis=0, tiled=True
+    )
+    everyone = gathered[:, :width]
+    shares = gathered[:, width : width + 2 * experts].astype(jnp.float32)
     me = lax.axis_index("expert")
     partial = 0.0
     for e in range(local):
-        mine = jnp.arange(experts, dtype=jnp.int32) == me * local + e
-        scale = jnp.sum(jnp.where(mine[None, :], dense_all, 0.0), axis=1, keepdims=True)
+        mine = jnp.arange(2 * experts, dtype=jnp.int32) % experts == me * local + e
+        scale = jnp.sum(jnp.where(mine[None, :], shares, 0.0), axis=1, keepdims=True)
         gate_values = jnp.dot(everyone, w_gate[e], preferred_element_type=jnp.float32)
         up_values = jnp.dot(everyone, w_up[e], preferred_element_type=jnp.float32)
         activated = (jax.nn.silu(gate_values) * up_values).astype(jnp.bfloat16)
         partial = partial + scale * jnp.dot(
             activated, w_down[e], preferred_element_type=jnp.float32
         )
-    mixture = lax.psum_scatter(
-        partial.astype(jnp.bfloat16), "expert", scatter_dimension=0, tiled=True
-    )
-    thinker_out = (hidden.astype(jnp.float32) + mixture.astype(jnp.float32)).astype(jnp.bfloat16)
-    voice_in = rms_scaled(thinker_out, talk_gain).astype(jnp.bfloat16)
-    pick = talker_pick(talker_owner, speaking, devices, capacity)
-    outgoing_voice = (
-        jnp.dot(pick, voice_in, preferred_element_type=jnp.float32)
-        .astype(jnp.bfloat16)
-        .reshape(devices, capacity, width)
-    )
-    arrived = lax.all_to_all(outgoing_voice, "expert", split_axis=0, concat_axis=0, tiled=True)
-    projected = jnp.dot(
-        arrived.reshape(devices * capacity, width), w_talk, preferred_element_type=jnp.float32
-    )
-    talker_out = (codec_state.astype(jnp.float32) + projected).astype(jnp.bfloat16)
-    return (thinker_out, talker_out)
+    return finish(
+        devices,
+        capacity,
+        partial.astype(jnp.bfloat16),
+        hidden,
+        picks,
+        talk_gain,
+        codec_state,
+        w_talk,
+    )
 
 
 def solution(mesh):

time: 184 us -> 147 us (0.80)
  waiting for transfers between devices: 88.8 us -> 49.1 us
  Pallas kernels: 14.4 us -> 52 us
  blocking collectives: 37.1 us -> 0 us
  local copies, waits for them, and re-layouts: 8.01 us -> 11 us
  matrix products: 19.6 us -> 17.3 us
  other arithmetic: 1.23 us -> 3.49 us
    reduce_scatter x1 -> x0, waiting for transfers between devices: 64.4 us -> none  [body(): lax.psum_scatter(partial.astype(jnp.bfloat16), 'expert', scatter_dimensio...]
    pallas_call x0 -> x1, Pallas kernels: none -> 38.1 us  [finish(): pl.pallas_call(functools.partial(finish_kernel, n, capacity), out_shape=(...]
    all_gather x1, waiting for transfers between devices: 24.4 us -> 49.1 us  [body(): lax.all_gather(jnp.concatenate([normed, riders], axis=1), 'expert', axis=...]
    all_gather x1 -> x0, blocking collectives: 23.6 us -> none  [body(): dense_all = lax.all_gather(dense, 'expert', axis=0, tiled=True)]
    all_to_all x1 -> x0, blocking collectives: 13.5 us -> none  [body(): lax.all_to_all(outgoing_voice, 'expert', split_axis=0, concat_axis=0, til...]
    unnamed x28 -> x23, local copies, waits for them, and re-layouts: 7.07 us -> 10.1 us
  transfers between devices with their start and end apart: 2 -> 1, of which waited for: 2 -> 1; matrix products, arithmetic and copies ran while one was open for 0% -> 1% of each run, Pallas kernels for 0% -> 0%
where the time goes in v1:
time: 147 us
  Pallas kernels  52 us (35%)
  waiting for transfers between devices  49.1 us (33%)
  matrix products  17.3 us (12%)
  between operations  14.1 us (10%)
  local copies, waits for them, and re-layouts  11 us (7%)
  other arithmetic  3.49 us (2%)
    all_gather x1, waiting for transfers between devices, body(): lax.all_gather(jnp.concatenate([normed, riders], axis=1), 'expert', axis=...  49.1 us
    pallas_call x1, Pallas kernels, finish(): pl.pallas_call(functools.partial(finish_kernel, n, capacity), out_shape=(...  38.1 us
    pallas_call x1, Pallas kernels, attend(): pl.pallas_call(functools.partial(attend_kernel, kv_width // (2 * HD), pag...  13.9 us
    dot_general x1, matrix products, body(): jnp.dot(activated, w_down[e], preferred_element_type=jnp.float32)  10.5 us
    unnamed x23, local copies, waits for them, and re-layouts  10.1 us
    dot_general x1, matrix products, body(): jnp.dot(everyone, w_gate[e], preferred_element_type=jnp.float32)  6.64 us
  transfers between devices with their start and end apart: 1, of which 1 were waited for; matrix products, arithmetic and copies ran while one was open for 1% of the time, Pallas kernels for 0%

profile of v1, /device:TPU:0, one launch (start us, length us, event | category | flops | bytes accessed | tf_op | source)
XLA Modules:
  0.0 147.0 jit_solution(3024322229523684434)
XLA Ops:
  7.2 0.0 all-gather.2.cloned.1.call-start
  7.2 0.8 select_reduce_fusion.1
  8.1 0.1 copy.31
  8.2 0.8 copy.29.table_ref
  9.0 0.8 copy.30.len_ref
  9.7 1.9 %copy-done.2 = bf16[192,16,512]{2,1,0:T(8,128)(2,1)S(1)} copy-done((bf16[192,16,512]{2,1,0:T(8,128)(2,1)S(1)}, bf16[192,16,512]{2,1,0:T(8,128)(2,1)}, u32[]{:S(2)}) %copy-start.2) | copy-done | bytes 3145752
  11.6 1.0 copy-done.3
  12.6 0.9 copy-done.4
  13.6 0.9 copy-done.5
  14.5 0.7 copy-done.6
  15.1 13.9 %shard_map.185 = (bf16[96,1024]{1,0:T(8,128)(2,1)S(1)}, bf16[96,1024]{1,0:T(8,128)(2,1)S(1)}) custom-call(bf16[96,2048]{1,0:T(8,128)(2,1)S(1)} %copy-done.3, bf16[3072,512]{1,0:T(8,128)(2,1)S(1)} %bitcast.16, bf16[96,512]{1,0:T(8,128)(2,1)S(1)} %copy-done.5, s32[96,16]{1,0:T(8,128)S(1)} %copy.29.table_ref, s32[96,1]{1,0:T(8,128)S(1)} %copy.30.len_ref, ...), custom_call_target="tpu_custom_call" | custom-call | flops 2415919104 | bytes 8126464 | tf_op jit(solution)/shard_map/pallas_call | solution.py:112
  29.1 0.7 copy-done.1
  29.7 0.7 fusion.12
  30.4 0.0 all-gather.2.cloned.1.call-update
  30.5 0.2 fusion.10
  30.7 0.1 iota_compare_fusion.1
  30.7 0.7 add_convert_fusion.picks_ref
  31.4 49.1 %all-gather.2.cloned.1.call-done = bf16[1536,1152]{1,0:T(8,128)(2,1)} async-done(((bf16[96,1152]{1,0:T(8,128)(2,1)}), bf16[1536,1152]{1,0:T(8,128)(2,1)}) %all-gather.2.cloned.1.call-update) | async-done | bytes 3538960 | tf_op jit(solution)/shard_map/all_gather | solution.py:363
  80.5 6.6 %fusion.1 = f32[1536,768]{1,0:T(8,128)} fusion(bf16[1536,1152]{1,0:T(8,128)(2,1)} %all-gather.2.cloned.1.call-done, bf16[1,1024,768]{2,1,0:T(8,128)(2,1)S(1)} %copy-done.9), kind=kOutput, calls=%fused_computation.3 | convolution fusion | flops 2415919104 | bytes 9437184 | tf_op jit(solution)/shard_map/dot_general | solution.py:373
  87.2 1.2 select_reduce_fusion
  88.3 10.5 %multiply_convert_fusion = bf16[1536,1024]{1,0:T(8,128)(2,1)} fusion(f32[1536]{0:T(1024)S(1)} %select_reduce_fusion, bf16[1,768,1024]{2,1,0:T(8,128)(2,1)S(1)} %copy-done, f32[1536,768]{1,0:T(8,128)} %fusion.1, bf16[1536,1152]{1,0:T(8,128)(2,1)} %all-gather.2.cloned.1.call-done, bf16[1,1024,768]{2,1,0:T(8,128)(2,1)} %param.27), kind=kOutput, calls=%fused_computation | convolution fusion | flops 4842061824 | bytes 14161920 | tf_op jit(solution)/shard_map/dot_general | solution.py:376
  98.8 38.1 %shard_map.186 = (bf16[96,1024]{1,0:T(8,128)(2,1)}, bf16[96,1024]{1,0:T(8,128)(2,1)}) custom-call(bf16[16,96,1024]{2,1,0:T(8,128)(2,1)} %bitcast.18, bf16[96,1024]{1,0:T(8,128)(2,1)} %copy-done.1, bf16[2,256,96]{2,1,0:T(8,128)(2,1)} %add_convert_fusion.picks_ref, f32[1,1024]{1,0:T(1,128)} %bitcast.19, bf16[96,1024]{1,0:T(8,128)(2,1)} %codec_ref.1, ...), custom_call_target="tpu_custom_call" | custom-call | tf_op jit(solution)/shard_map/pallas_call | solution.py:277
  136.9 1.6 %copy.34 = bf16[96,1024]{1,0:T(8,128)(2,1)} copy(bf16[96,1024]{1,0:T(8,128)(2,1)} %get-tuple-element.14) | data formatting | bytes 393216
  138.6 1.6 %copy.35 = bf16[96,1024]{1,0:T(8,128)(2,1)} copy(bf16[96,1024]{1,0:T(8,128)(2,1)} %get-tuple-element.15) | data formatting | bytes 393216
  (19 shorter events, 0.1 us)
Async XLA Ops:
  7.2 81.2 %copy-start = (bf16[1,768,1024]{2,1,0:T(8,128)(2,1)S(1)}, bf16[1,768,1024]{2,1,0:T(8,128)(2,1)}, u32[]{:S(2)}) copy-start(bf16[1,768,1024]{2,1,0:T(8,128)(2,1)} %param.28) | copy-start | bytes 4718596
  7.2 73.3 %all-gather.2.cloned.1.call-start = ((), (), s32[]{:S(2)}) async-start(), calls=%async_computation | async-start | bytes 3760128 | tf_op jit(solution)/shard_map/all_gather | solution.py:363
  9.7 1.9 %copy-start.2 = (bf16[192,16,512]{2,1,0:T(8,128)(2,1)S(1)}, bf16[192,16,512]{2,1,0:T(8,128)(2,1)}, u32[]{:S(2)}) copy-start(bf16[192,16,512]{2,1,0:T(8,128)(2,1)} %param.19) | copy-start | bytes 9437188
  11.6 1.0 copy-start.3
  12.6 0.9 copy-start.4
  13.6 0.9 copy-start.5
  14.4 0.7 copy-start.6
  15.1 15.3 %copy-start.8 = (s32[96]{0:T(128)S(1)}, s32[96]{0:T(128)}, u32[]{:S(2)}) copy-start(s32[96]{0:T(128)} %param.32) | copy-start | bytes 1156
  15.1 15.4 %copy-start.7 = (s32[96]{0:T(128)S(1)}, s32[96]{0:T(128)}, u32[]{:S(2)}) copy-start(s32[96]{0:T(128)} %param.31) | copy-start | bytes 1156
  15.1 65.4 %copy-start.9 = (bf16[1,1024,768]{2,1,0:T(8,128)(2,1)S(1)}, bf16[1,1024,768]{2,1,0:T(8,128)(2,1)}, u32[]{:S(2)}) copy-start(bf16[1,1024,768]{2,1,0:T(8,128)(2,1)} %param.26) | copy-start | bytes 4718596
  29.1 0.7 copy-start.1
Sparse Core Ops, SparseCore 0:
  30.6 49.8 all-gather.1

commit v2 on v1

--- a/solution.py
+++ b/solution.py
@@ -143,6 +143,68 @@
         out = out + stride * ((1 - bit) if bits & stride else bit)
         stride *= 2
     return out
+
+
+def gather_kernel(n, own_ref, out_ref, send_sem, recv_sem):
+    wide = own_ref.shape[1]
+    first = -(-wide // 256) * 128
+    spans = ((0, first), (first, wide - first))
+    me = lax.axis_index("expert")
+    strides = [1 << b for b in range(n.bit_length() - 1)]
+    orders = (strides[::-1], strides[1:2] + strides[:1:-1] + strides[:1])
+    barrier = pltpu.get_barrier_semaphore()
+    for s in strides:
+        pl.semaphore_signal(
+            barrier,
+            inc=1,
+            device_id={"expert": flipped(me, s, n)},
+            device_id_type=pl.DeviceIdType.MESH,
+        )
+    out_ref[pl.ds(me, 1)] = own_ref[...][None]
+    pl.semaphore_wait(barrier, len(strides))
+
+    def message(half, m, s):
+        block = out_ref.at[flipped(me, m - s, n), :, pl.ds(*spans[half])]
+        return pltpu.make_async_remote_copy(
+            src_ref=block,
+            dst_ref=block,
+            send_sem=send_sem.at[half, m],
+            recv_sem=recv_sem.at[half, m],
+            device_id={"expert": flipped(me, s, n)},
+            device_id_type=pl.DeviceIdType.MESH,
+        )
+
+    sent, held, waited = {}, ([0], [0]), set()
+    for k in range(len(strides)):
+        added = ([], [])
+        for place in range(1 << k):
+            for half in range(2):
+                s, r = orders[half][k], held[half][place]
+                if r and (half, r) not in waited:
+                    sent[half, r].wait_recv()
+                    waited.add((half, r))
+                sent[half, r + s] = message(half, r + s, s)
+                sent[half, r + s].start()
+                added[half].append(r + s)
+        for half in range(2):
+            held[half].extend(added[half])
+    for key, copy in sent.items():
+        if key not in waited:
+            copy.wait_recv()
+        copy.wait_send()
+
+
+def gather_rows(n, own):
+    return pl.pallas_call(
+        functools.partial(gather_kernel, n),
+        out_shape=jax.ShapeDtypeStruct((n,) + own.shape, own.dtype),
+        in_specs=[pl.BlockSpec(memory_space=pltpu.VMEM)],
+        out_specs=pl.BlockSpec(memory_space=pltpu.VMEM),
+        scratch_shapes=[pltpu.SemaphoreType.DMA((2, n)), pltpu.SemaphoreType.DMA((2, n))],
+        compiler_params=pltpu.CompilerParams(
+            collective_id=1, has_side_effects=True, vmem_limit_bytes=40 * 1024 * 1024
+        ),
+    )(own).reshape(n * own.shape[0], own.shape[1])
 
 
 def finish_kernel(
@@ -360,9 +422,7 @@
     hidden, normed = attend(
         queries, kv_cache, new_kv, page_table, ctx_len, resid, w_out, moe_gain
     )
-    gathered = lax.all_gather(
-        jnp.concatenate([normed, riders], axis=1), "expert", axis=0, tiled=True
-    )
+    gathered = gather_rows(devices, jnp.concatenate([normed, riders], axis=1))
     everyone = gathered[:, :width]
     shares = gathered[:, width : width + 2 * experts].astype(jnp.float32)
     me = lax.axis_index("expert")

time: 147 us -> 110 us (0.75)
  waiting for transfers between devices: 49.1 us -> 0 us
  Pallas kernels: 52 us -> 80.8 us
  between operations: 14.1 us -> 0.79 us
  matrix products: 17.3 us -> 14.4 us
    all_gather x1 -> x0, waiting for transfers between devices: 49.1 us -> none  [body(): lax.all_gather(jnp.concatenate([normed, riders], axis=1), 'expert', axis=...]
    pallas_call x0 -> x1, Pallas kernels: none -> 28.1 us  [gather_rows(): pl.pallas_call(functools.partial(gather_kernel, n), out_shape=jax.ShapeDt...]
    dot_general x1, matrix products: 6.64 us -> 4.21 us  [body(): jnp.dot(everyone, w_gate[e], preferred_element_type=jnp.float32)]
    unnamed x23 -> x27, local copies, waits for them, and re-layouts: 10.1 us -> 9.46 us
  transfers between devices with their start and end apart: 1 -> 0, of which waited for: 1 -> 0; matrix products, arithmetic and copies ran while one was open for 1% -> 0% of each run, Pallas kernels for 0% -> 0%
where the time goes in v2:
time: 110 us; the launch traced here: 109 us
  Pallas kernels  80.8 us (73%)
  matrix products  14.4 us (13%)
  local copies, waits for them, and re-layouts  10.3 us (9%)
  other arithmetic  2.82 us (3%)
    pallas_call x1, Pallas kernels, finish(): pl.pallas_call(functools.partial(finish_kernel, n, capacity), out_shape=(...  38.8 us
    pallas_call x1, Pallas kernels, gather_rows(): pl.pallas_call(functools.partial(gather_kernel, n), out_shape=jax.ShapeDt...  28.1 us
    pallas_call x1, Pallas kernels, attend(): pl.pallas_call(functools.partial(attend_kernel, kv_width // (2 * HD), pag...  13.8 us
    dot_general x1, matrix products, body(): jnp.dot(activated, w_down[e], preferred_element_type=jnp.float32)  10 us
    unnamed x27, local copies, waits for them, and re-layouts  9.46 us
    dot_general x1, matrix products, body(): jnp.dot(everyone, w_gate[e], preferred_element_type=jnp.float32)  4.21 us

profile of v2, /device:TPU:0, one launch (start us, length us, event | category | flops | bytes accessed | tf_op | source)
XLA Modules:
  0.0 109.1 jit_solution(8558518630670002156)
XLA Ops:
  0.6 0.0 copy-start
  0.6 0.8 select_reduce_fusion.1
  1.5 0.1 copy.31
  1.6 0.8 copy.29.table_ref
  2.4 0.8 copy.30.len_ref
  3.2 1.9 %copy-done.3 = bf16[192,16,512]{2,1,0:T(8,128)(2,1)S(1)} copy-done((bf16[192,16,512]{2,1,0:T(8,128)(2,1)S(1)}, bf16[192,16,512]{2,1,0:T(8,128)(2,1)}, u32[]{:S(2)}) %copy-start.3) | copy-done | bytes 3145752
  5.1 1.0 copy-done.4
  6.1 0.9 copy-done.5
  7.0 0.9 copy-done.6
  7.9 0.7 copy-done.7
  8.6 13.8 %shard_map.185 = (bf16[96,1024]{1,0:T(8,128)(2,1)S(1)}, bf16[96,1024]{1,0:T(8,128)(2,1)S(1)}) custom-call(bf16[96,2048]{1,0:T(8,128)(2,1)S(1)} %copy-done.4, bf16[3072,512]{1,0:T(8,128)(2,1)S(1)} %bitcast.20, bf16[96,512]{1,0:T(8,128)(2,1)S(1)} %copy-done.6, s32[96,16]{1,0:T(8,128)S(1)} %copy.29.table_ref, s32[96,1]{1,0:T(8,128)S(1)} %copy.30.len_ref, ...), custom_call_target="tpu_custom_call" | custom-call | flops 2415919104 | bytes 8126464 | tf_op jit(solution)/shard_map/pallas_call | solution.py:112
  22.4 0.0 copy-start.10
  22.4 28.1 %shard_map.186 = bf16[16,96,1152]{2,1,0:T(8,128)(2,1)S(1)} custom-call(bf16[96,1152]{1,0:T(8,128)(2,1)S(1)} %fusion.12.own_ref), custom_call_target="tpu_custom_call" | custom-call | tf_op jit(solution)/shard_map/pallas_call | solution.py:198
  50.6 0.0 copy-start.11
  50.6 4.2 %fusion.1 = f32[1536,768]{1,0:T(8,128)} fusion(bf16[1536,1152]{1,0:T(8,128)(2,1)S(1)} %bitcast.17, bf16[1,1024,768]{2,1,0:T(8,128)(2,1)S(1)} %copy-done.10), kind=kOutput, calls=%fused_computation.3 | convolution fusion | flops 2415919104 | bytes 9437184 | tf_op jit(solution)/shard_map/dot_general | solution.py:433
  54.8 1.2 %select_reduce_fusion = f32[1536]{0:T(1024)S(1)} fusion(bf16[1536,1152]{1,0:T(8,128)(2,1)} %bitcast.18, pred[32]{0:T(512)(128)(4,1)S(1)} %fusion.18), kind=kLoop, calls=%fused_computation.10 | loop fusion | flops 145920 | bytes 104480 | tf_op jit(solution)/shard_map/reduce_sum | solution.py:432
  56.0 0.0 copy-start.9
  56.0 10.0 %multiply_convert_fusion = bf16[1536,1024]{1,0:T(8,128)(2,1)} fusion(f32[1536]{0:T(1024)S(1)} %select_reduce_fusion, bf16[1,768,1024]{2,1,0:T(8,128)(2,1)S(1)} %copy-done, f32[1536,768]{1,0:T(8,128)} %fusion.1, bf16[1536,1152]{1,0:T(8,128)(2,1)} %bitcast.19, bf16[1,1024,768]{2,1,0:T(8,128)(2,1)S(1)} %copy-done.11), kind=kOutput, calls=%fused_computation | convolution fusion | flops 4842061824 | bytes 14161920 | tf_op jit(solution)/shard_map/dot_general | solution.py:436
  66.1 0.2 fusion.10
  66.3 0.1 iota_compare_fusion.1
  66.3 0.7 add_convert_fusion.picks_ref
  67.0 38.8 %shard_map.187 = (bf16[96,1024]{1,0:T(8,128)(2,1)}, bf16[96,1024]{1,0:T(8,128)(2,1)}) custom-call(bf16[16,96,1024]{2,1,0:T(8,128)(2,1)} %bitcast.22, bf16[96,1024]{1,0:T(8,128)(2,1)} %copy-done.2, bf16[2,256,96]{2,1,0:T(8,128)(2,1)} %add_convert_fusion.picks_ref, f32[1,1024]{1,0:T(1,128)} %bitcast.23, bf16[96,1024]{1,0:T(8,128)(2,1)} %codec_ref.1, ...), custom_call_target="tpu_custom_call" | custom-call | tf_op jit(solution)/shard_map/pallas_call | solution.py:339
  105.8 1.6 %copy.34 = bf16[96,1024]{1,0:T(8,128)(2,1)} copy(bf16[96,1024]{1,0:T(8,128)(2,1)} %get-tuple-element.14) | data formatting | bytes 393216
  107.5 1.6 %copy.35 = bf16[96,1024]{1,0:T(8,128)(2,1)} copy(bf16[96,1024]{1,0:T(8,128)(2,1)} %get-tuple-element.15) | data formatting | bytes 393216
  (21 shorter events, 0.1 us)
Async XLA Ops:
  0.6 55.4 %copy-start = (bf16[1,768,1024]{2,1,0:T(8,128)(2,1)S(1)}, bf16[1,768,1024]{2,1,0:T(8,128)(2,1)}, u32[]{:S(2)}) copy-start(bf16[1,768,1024]{2,1,0:T(8,128)(2,1)} %param.28) | copy-start | bytes 4718596
  3.2 1.9 %copy-start.3 = (bf16[192,16,512]{2,1,0:T(8,128)(2,1)S(1)}, bf16[192,16,512]{2,1,0:T(8,128)(2,1)}, u32[]{:S(2)}) copy-start(bf16[192,16,512]{2,1,0:T(8,128)(2,1)} %param.19) | copy-start | bytes 9437188
  5.1 1.0 copy-start.4
  6.1 0.9 copy-start.5
  7.0 0.9 copy-start.6
  7.9 0.7 copy-start.7
  22.4 32.4 %copy-start.2 = (bf16[96,1024]{1,0:T(8,128)(2,1)}, bf16[96,1024]{1,0:T(8,128)(2,1)S(1)}, u32[]{:S(2)}) copy-start(bf16[96,1024]{1,0:T(8,128)(2,1)S(1)} %get-tuple-element.5.hidden_ref) | copy-start | bytes 589828
  22.4 28.2 %copy-start.10 = (bf16[1,1024,768]{2,1,0:T(8,128)(2,1)S(1)}, bf16[1,1024,768]{2,1,0:T(8,128)(2,1)}, u32[]{:S(2)}) copy-start(bf16[1,1024,768]{2,1,0:T(8,128)(2,1)} %param.26) | copy-start | bytes 4718596
  50.6 4.2 %copy-start.1 = (bf16[16,96,1152]{2,1,0:T(8,128)(2,1)}, bf16[16,96,1152]{2,1,0:T(8,128)(2,1)S(1)}, u32[]{:S(2)}) copy-start(bf16[16,96,1152]{2,1,0:T(8,128)(2,1)S(1)} %shard_map.186) | copy-start | bytes 10616836
  50.6 5.4 %copy-start.11 = (bf16[1,1024,768]{2,1,0:T(8,128)(2,1)S(1)}, bf16[1,1024,768]{2,1,0:T(8,128)(2,1)}, u32[]{:S(2)}) copy-start(bf16[1,1024,768]{2,1,0:T(8,128)(2,1)} %param.27) | copy-start | bytes 4718596
  56.0 10.1 %copy-start.9 = (s32[96]{0:T(128)S(1)}, s32[96]{0:T(128)}, u32[]{:S(2)}) copy-start(s32[96]{0:T(128)} %param.32) | copy-start | bytes 1156
  56.0 10.1 %copy-start.8 = (s32[96]{0:T(128)S(1)}, s32[96]{0:T(128)}, u32[]{:S(2)}) copy-start(s32[96]{0:T(128)} %param.31) | copy-start | bytes 1156

commit v3 on v2

--- a/solution.py
+++ b/solution.py
@@ -271,18 +271,20 @@
 
     sent = {}
     for k in range(len(strides)):
+        todo = []
         for half in range(2):
-            todo = [r for r in range(1, n) if step_of(half, r) == k]
+            now = [r for r in range(1, n) if step_of(half, r) == k]
             nearer = orders[half][k + 1 :]
-            todo.sort(key=lambda r: [-((r & s) > 0) for s in nearer])
-            for r in todo:
-                if k == 0:
-                    source = part_ref.at[flipped(me, r, n), :, pl.ds(half * cols, cols)]
-                else:
-                    stage[half, r] = summed(half, r, k).astype(jnp.bfloat16)
-                    source = stage.at[half, r]
-                sent[half, r] = message(half, r, source)
-                sent[half, r].start()
+            now.sort(key=lambda r: [-((r & s) > 0) for s in nearer])
+            todo.append([(half, r) for r in now])
+        for half, r in [one for pair in zip(*todo) for one in pair]:
+            if k == 0:
+                source = part_ref.at[flipped(me, r, n), :, pl.ds(half * cols, cols)]
+            else:
+                stage[half, r] = summed(half, r, k).astype(jnp.bfloat16)
+                source = stage.at[half, r]
+            sent[half, r] = message(half, r, source)
+            sent[half, r].start()
     mixture = jnp.concatenate([summed(half, 0, len(strides)) for half in range(2)], axis=1)
     thinker = (hidden_ref[...].astype(jnp.float32) + mixture).astype(jnp.bfloat16)
     thinker_ref[...] = thinker

time: 110 us -> 109 us (level)
  no operation moved by 1% of the time
where the time goes in v3:
time: 109 us; the launch traced here: 108 us
  Pallas kernels  79.8 us (73%)
  matrix products  14.4 us (13%)
  local copies, waits for them, and re-layouts  10.3 us (9%)
  other arithmetic  2.82 us (3%)
    pallas_call x1, Pallas kernels, finish(): pl.pallas_call(functools.partial(finish_kernel, n, capacity), out_shape=(...  37.9 us
    pallas_call x1, Pallas kernels, gather_rows(): pl.pallas_call(functools.partial(gather_kernel, n), out_shape=jax.ShapeDt...  28.1 us
    pallas_call x1, Pallas kernels, attend(): pl.pallas_call(functools.partial(attend_kernel, kv_width // (2 * HD), pag...  13.8 us
    dot_general x1, matrix products, body(): jnp.dot(activated, w_down[e], preferred_element_type=jnp.float32)  10 us
    unnamed x27, local copies, waits for them, and re-layouts  9.46 us
    dot_general x1, matrix products, body(): jnp.dot(everyone, w_gate[e], preferred_element_type=jnp.float32)  4.21 us

profile of v3, /device:TPU:0, one launch (start us, length us, event | category | flops | bytes accessed | tf_op | source)
XLA Modules:
  0.0 108.1 jit_solution(15783870573137069477)
XLA Ops:
  0.6 0.0 copy-start
  0.6 0.8 select_reduce_fusion.1
  1.5 0.1 copy.31
  1.6 0.8 copy.29.table_ref
  2.4 0.8 copy.30.len_ref
  3.2 1.9 %copy-done.3 = bf16[192,16,512]{2,1,0:T(8,128)(2,1)S(1)} copy-done((bf16[192,16,512]{2,1,0:T(8,128)(2,1)S(1)}, bf16[192,16,512]{2,1,0:T(8,128)(2,1)}, u32[]{:S(2)}) %copy-start.3) | copy-done | bytes 3145752
  5.1 1.0 copy-done.4
  6.1 0.9 copy-done.5
  7.0 0.9 copy-done.6
  7.9 0.7 copy-done.7
  8.6 13.8 %shard_map.185 = (bf16[96,1024]{1,0:T(8,128)(2,1)S(1)}, bf16[96,1024]{1,0:T(8,128)(2,1)S(1)}) custom-call(bf16[96,2048]{1,0:T(8,128)(2,1)S(1)} %copy-done.4, bf16[3072,512]{1,0:T(8,128)(2,1)S(1)} %bitcast.20, bf16[96,512]{1,0:T(8,128)(2,1)S(1)} %copy-done.6, s32[96,16]{1,0:T(8,128)S(1)} %copy.29.table_ref, s32[96,1]{1,0:T(8,128)S(1)} %copy.30.len_ref, ...), custom_call_target="tpu_custom_call" | custom-call | flops 2415919104 | bytes 8126464 | tf_op jit(solution)/shard_map/pallas_call | solution.py:112
  22.4 0.0 copy-start.2
  22.4 0.0 copy-start.10
  22.4 28.1 %shard_map.186 = bf16[16,96,1152]{2,1,0:T(8,128)(2,1)S(1)} custom-call(bf16[96,1152]{1,0:T(8,128)(2,1)S(1)} %fusion.12.own_ref), custom_call_target="tpu_custom_call" | custom-call | tf_op jit(solution)/shard_map/pallas_call | solution.py:198
  50.6 4.2 %fusion.1 = f32[1536,768]{1,0:T(8,128)} fusion(bf16[1536,1152]{1,0:T(8,128)(2,1)S(1)} %bitcast.17, bf16[1,1024,768]{2,1,0:T(8,128)(2,1)S(1)} %copy-done.10), kind=kOutput, calls=%fused_computation.3 | convolution fusion | flops 2415919104 | bytes 9437184 | tf_op jit(solution)/shard_map/dot_general | solution.py:435
  54.8 1.2 %select_reduce_fusion = f32[1536]{0:T(1024)S(1)} fusion(bf16[1536,1152]{1,0:T(8,128)(2,1)} %bitcast.18, pred[32]{0:T(512)(128)(4,1)S(1)} %fusion.18), kind=kLoop, calls=%fused_computation.10 | loop fusion | flops 145920 | bytes 104480 | tf_op jit(solution)/shard_map/reduce_sum | solution.py:434
  56.0 0.0 copy-start.9
  56.0 10.0 %multiply_convert_fusion = bf16[1536,1024]{1,0:T(8,128)(2,1)} fusion(f32[1536]{0:T(1024)S(1)} %select_reduce_fusion, bf16[1,768,1024]{2,1,0:T(8,128)(2,1)S(1)} %copy-done, f32[1536,768]{1,0:T(8,128)} %fusion.1, bf16[1536,1152]{1,0:T(8,128)(2,1)} %bitcast.19, bf16[1,1024,768]{2,1,0:T(8,128)(2,1)S(1)} %copy-done.11), kind=kOutput, calls=%fused_computation | convolution fusion | flops 4842061824 | bytes 14161920 | tf_op jit(solution)/shard_map/dot_general | solution.py:438
  66.1 0.2 fusion.10
  66.3 0.1 iota_compare_fusion.1
  66.3 0.7 add_convert_fusion.picks_ref
  67.0 37.9 %shard_map.187 = (bf16[96,1024]{1,0:T(8,128)(2,1)}, bf16[96,1024]{1,0:T(8,128)(2,1)}) custom-call(bf16[16,96,1024]{2,1,0:T(8,128)(2,1)} %bitcast.22, bf16[96,1024]{1,0:T(8,128)(2,1)} %copy-done.2, bf16[2,256,96]{2,1,0:T(8,128)(2,1)} %add_convert_fusion.picks_ref, f32[1,1024]{1,0:T(1,128)} %bitcast.23, bf16[96,1024]{1,0:T(8,128)(2,1)} %codec_ref.1, ...), custom_call_target="tpu_custom_call" | custom-call | tf_op jit(solution)/shard_map/pallas_call | solution.py:341
  104.9 1.6 %copy.34 = bf16[96,1024]{1,0:T(8,128)(2,1)} copy(bf16[96,1024]{1,0:T(8,128)(2,1)} %get-tuple-element.14) | data formatting | bytes 393216
  106.5 1.6 %copy.35 = bf16[96,1024]{1,0:T(8,128)(2,1)} copy(bf16[96,1024]{1,0:T(8,128)(2,1)} %get-tuple-element.15) | data formatting | bytes 393216
  (21 shorter events, 0.1 us)
Async XLA Ops:
  0.6 55.4 %copy-start = (bf16[1,768,1024]{2,1,0:T(8,128)(2,1)S(1)}, bf16[1,768,1024]{2,1,0:T(8,128)(2,1)}, u32[]{:S(2)}) copy-start(bf16[1,768,1024]{2,1,0:T(8,128)(2,1)} %param.28) | copy-start | bytes 4718596
  3.2 1.9 %copy-start.3 = (bf16[192,16,512]{2,1,0:T(8,128)(2,1)S(1)}, bf16[192,16,512]{2,1,0:T(8,128)(2,1)}, u32[]{:S(2)}) copy-start(bf16[192,16,512]{2,1,0:T(8,128)(2,1)} %param.19) | copy-start | bytes 9437188
  5.1 1.0 copy-start.4
  6.1 0.9 copy-start.5
  7.0 0.9 copy-start.6
  7.9 0.7 copy-start.7
  22.4 32.4 %copy-start.2 = (bf16[96,1024]{1,0:T(8,128)(2,1)}, bf16[96,1024]{1,0:T(8,128)(2,1)S(1)}, u32[]{:S(2)}) copy-start(bf16[96,1024]{1,0:T(8,128)(2,1)S(1)} %get-tuple-element.5.hidden_ref) | copy-start | bytes 589828
  22.4 28.2 %copy-start.10 = (bf16[1,1024,768]{2,1,0:T(8,128)(2,1)S(1)}, bf16[1,1024,768]{2,1,0:T(8,128)(2,1)}, u32[]{:S(2)}) copy-start(bf16[1,1024,768]{2,1,0:T(8,128)(2,1)} %param.26) | copy-start | bytes 4718596
  50.6 4.2 %copy-start.1 = (bf16[16,96,1152]{2,1,0:T(8,128)(2,1)}, bf16[16,96,1152]{2,1,0:T(8,128)(2,1)S(1)}, u32[]{:S(2)}) copy-start(bf16[16,96,1152]{2,1,0:T(8,128)(2,1)S(1)} %shard_map.186) | copy-start | bytes 10616836
  50.6 5.4 %copy-start.11 = (bf16[1,1024,768]{2,1,0:T(8,128)(2,1)S(1)}, bf16[1,1024,768]{2,1,0:T(8,128)(2,1)}, u32[]{:S(2)}) copy-start(bf16[1,1024,768]{2,1,0:T(8,128)(2,1)} %param.27) | copy-start | bytes 4718596
  56.0 10.1 %copy-start.9 = (s32[96]{0:T(128)S(1)}, s32[96]{0:T(128)}, u32[]{:S(2)}) copy-start(s32[96]{0:T(128)} %param.32) | copy-start | bytes 1156
  56.0 10.1 %copy-start.8 = (s32[96]{0:T(128)S(1)}, s32[96]{0:T(128)}, u32[]{:S(2)}) copy-start(s32[96]{0:T(128)} %param.31) | copy-start | bytes 1156
